TPU v7x, 512 devices: a whole 4x8x8 slice. The times are simulated.
512 devices in a mesh: tm: 64 (over x, y, core), space: 8 (over z).
Axes of the slice: x: 4, y: 8, z: 8, core: 2. Of those that a mesh axis runs over, the one named last changes fastest.
Arguments:
- x_in: bfloat16 [128, 1024, 1024], P('tm', 'space'), may hold values from -6 to 6
- b_in: bfloat16 [128, 1024, 128], P('tm', 'space'), may hold values from -0.625 to 0.625
- c_in: bfloat16 [128, 1024, 128], P('tm', 'space'), may hold values from -0.625 to 0.625
- decay_log: float32 [128, 1024, 16], P('tm', 'space'), as said below
- qkv: bfloat16 [128, 1024, 3072], P('tm', 'space'), as said below
- block_of: int32 [128, 1024], P('tm', 'space'), may hold values from 0 to 31, as said below
- norm_gain: float32 [1024], replicated, may hold values from 0.1 to 1.9
Outputs:
- mixed: bfloat16 [128, 1024, 1024], P('tm', 'space')
Inputs may be any that keep to these rules, and one draw needn't show every extreme that they name: `block_of`: blocks o*4 to (o+1)*4 - 1 belong to space index o. Of one frame's tile of 128 tokens at most 32 lie in the blocks of one space index, and in every frame some space index holds exactly 32 tokens from every tile. `decay_log`: log decays, never positive. `qkv`: queries, keys and values, each 16 heads of 64 features.
All inputs are finite; a program needn't handle non-finite values.
Results may differ from a plain program's by a relative error of at most 0.005.
Values may be sent and summed in bfloat16 or wider, within the bound.
A program may use at most 128 MiB of HBM per device.

v0:
```python
import jax
import jax.numpy as jnp
from jax import lax
from jax.sharding import PartitionSpec as P

BLK_DEV = 4


def carried_in(x, axis, combine, identity):
    peers, mine = (lax.axis_size(axis), lax.axis_index(axis))
    everything = jax.tree.map(lambda part: lax.all_gather(part, axis), x)
    start = jax.tree.map(
        lambda part, zero: jnp.broadcast_to(jnp.asarray(zero, part.dtype), part.shape), x, identity
    )

    def step(k, before):
        reached = k < mine
        new = combine(before, jax.tree.map(lambda part: part[k], everything))
        return jax.tree.map(lambda a, b: jnp.where(reached, a, b), new, before)

    return lax.fori_loop(0, peers, step, start)


def block_inside(running, values_x, values_b, values_c):
    seq_len = running.shape[0]
    rows_at = lax.broadcasted_iota(jnp.int32, (seq_len, seq_len), 0)
    cols_at = lax.broadcasted_iota(jnp.int32, (seq_len, seq_len), 1)
    lower = cols_at <= rows_at
    gram = jnp.dot(values_c, values_b.T, preferred_element_type=jnp.float32)

    def block_one_head(pieces):
        head_running, head_x = pieces
        spread = head_running[:, None] - head_running[None, :]
        decay_mat = jnp.where(lower, jnp.exp(jnp.minimum(spread, 0.0)), 0.0)
        mixing = (gram * decay_mat).astype(jnp.bfloat16)
        return jnp.dot(mixing, head_x, preferred_element_type=jnp.float32)

    per_head = lax.map(block_one_head, (running.T, jnp.swapaxes(values_x, 0, 1)))
    return jnp.swapaxes(per_head, 0, 1)


def combine_states(earlier, later):
    return (earlier[0] * later[0], later[0][:, None, None] * earlier[1] + later[1])


def carry_in(running, values_x, values_b):
    tail = jnp.exp(running[-1][None, :] - running)
    weighted = (values_x.astype(jnp.float32) * tail[:, :, None]).astype(jnp.bfloat16)
    local_state = jnp.einsum("shp,sn->hpn", weighted, values_b, preferred_element_type=jnp.float32)
    block_decay = jnp.exp(running[-1])
    identity = (jnp.ones_like(block_decay), jnp.zeros_like(local_state))
    prefix = carried_in((block_decay, local_state), "tm", combine_states, identity)
    return prefix[1]


def attend(query, stochastic_seeds, values, query_labels, key_labels):
    scale = query.shape[-1] ** (-0.5)
    same = query_labels[:, None] == key_labels[None, :]

    def attend_one_head(pieces):
        head_q, head_k, head_v = pieces
        scores = jnp.dot(head_q, head_k.T, preferred_element_type=jnp.float32) * scale
        masked = jnp.where(same, scores, -1e30)
        highest = jnp.max(masked, axis=-1, keepdims=True)
        weights = jnp.where(same, jnp.exp(masked - highest), 0.0)
        probs = (weights / jnp.sum(weights, axis=-1, keepdims=True)).astype(jnp.bfloat16)
        return jnp.dot(probs, head_v, preferred_element_type=jnp.float32)

    per_head = lax.map(
        attend_one_head,
        (
            jnp.swapaxes(query, 0, 1),
            jnp.swapaxes(stochastic_seeds, 0, 1),
            jnp.swapaxes(values, 0, 1),
        ),
    )
    attended = jnp.swapaxes(per_head, 0, 1)
    return attended.reshape(query.shape[0], -1).astype(jnp.bfloat16)


def shards(x_in, b_in, c_in, decay_log, qkv, block_of, norm_gain):
    frames_here, tile_len, width = x_in.shape
    heads = decay_log.shape[2]
    head_size = width // heads
    state_size = b_in.shape[2]
    seq_len = frames_here * tile_len
    values_x = x_in.reshape(seq_len, heads, head_size)
    values_b = b_in.reshape(seq_len, state_size)
    values_c = c_in.reshape(seq_len, state_size)
    running = jnp.cumsum(decay_log.reshape(seq_len, heads), axis=0)
    inside = block_inside(running, values_x, values_b, values_c)
    entering = carry_in(running, values_x, values_b)
    from_carry = jnp.exp(running)[:, :, None] * jnp.einsum(
        "tn,hpn->thp", values_c.astype(jnp.float32), entering, precision=lax.Precision.HIGHEST
    )
    scanned = inside + from_carry
    mean_sq = jnp.mean(scanned * scanned, axis=-1, keepdims=True)
    normed = (scanned * lax.rsqrt(mean_sq + 1e-05)).reshape(
        frames_here, tile_len, width
    ) * norm_gain
    space_count = lax.axis_size("space")
    capacity = 2 * tile_len // space_count
    slot_count = space_count * capacity
    owners = block_of // BLK_DEV
    dest_hot = (
        owners[:, :, None] == jnp.arange(space_count, dtype=jnp.int32)[None, None, :]
    ).astype(jnp.int32)
    earlier_count = jnp.cumsum(dest_hot, axis=1) - dest_hot
    slot_rank = jnp.sum(earlier_count * dest_hot, axis=2)
    slot_at = owners * capacity + slot_rank
    place_int = (
        slot_at[:, :, None] == jnp.arange(slot_count, dtype=jnp.int32)[None, None, :]
    ).astype(jnp.int32)
    place = place_int.astype(jnp.bfloat16)
    send_rows = jnp.einsum("fts,ftd->fsd", place, qkv, preferred_element_type=jnp.float32).astype(
        jnp.bfloat16
    )
    send_rows = send_rows.reshape(frames_here, space_count, capacity, 3 * width)
    send_labels = jnp.sum(place_int * (block_of[:, :, None] + 1), axis=1) - 1
    send_labels = send_labels.reshape(frames_here, space_count, capacity)

    def slot_frame(pieces):
        rows, labels = pieces
        flat_rows = rows.reshape(-1, 3 * width)
        flat_labels = labels.reshape(-1)
        query = flat_rows[:, :width].reshape(-1, heads, head_size)
        stochastic_seeds = flat_rows[:, width : 2 * width].reshape(-1, heads, head_size)
        values = flat_rows[:, 2 * width :].reshape(-1, heads, head_size)
        blending_result = attend(query, stochastic_seeds, values, flat_labels, flat_labels)
        return blending_result.reshape(rows.shape[0], rows.shape[1], width)

    results = lax.map(
        slot_frame,
        (
            lax.all_to_all(send_rows, "space", split_axis=1, concat_axis=1, tiled=True),
            lax.all_to_all(send_labels, "space", split_axis=1, concat_axis=1, tiled=True),
        ),
    )
    returned = lax.all_to_all(results, "space", split_axis=1, concat_axis=1, tiled=True)
    returned = returned.reshape(frames_here, slot_count, width)
    attended = jnp.einsum("fts,fsd->ftd", place, returned, preferred_element_type=jnp.float32)
    return (normed + attended).astype(jnp.bfloat16)


def solution(mesh):
    return jax.shard_map(
        shards,
        mesh=mesh,
        in_specs=(
            P("tm", "space", None),
            P("tm", "space", None),
            P("tm", "space", None),
            P("tm", "space", None),
            P("tm", "space", None),
            P("tm", "space"),
            P(),
        ),
        out_specs=P("tm", "space", None),
        check_vma=False,
    )
```

profile of v0, /device:TPU:1, one launch (start us, length us, event | category | flops | bytes accessed | tf_op | source)
XLA Modules:
  0.0 292.2 jit_solution(13229542200931092354)
XLA Ops:
  9.6 1.8 mul.87
  11.4 1.3 copy.71
  12.7 1.3 multiply_convert_fusion.2
  14.0 1.4 convert_element_type.50
  17.9 10.9 %all-to-all-start.1 = ((s32[2,8,32]{2,0,1:T(2,128)}), s32[2,8,32]{2,0,1:T(2,128)S(1)}, u32[]{:S(2)}, u32[]{:S(2)}) async-start(s32[2,8,32]{2,0,1:T(2,128)} %copy.77), calls=%async_computation.1 | async-start | bytes 16384 | tf_op jit(solution)/shard_map/all_to_all | solution.py:136
  29.9 1.9 copy.76
  31.8 3.5 %all-to-all-done.1 = s32[2,8,32]{2,0,1:T(2,128)S(1)} async-done(((s32[2,8,32]{2,0,1:T(2,128)}), s32[2,8,32]{2,0,1:T(2,128)S(1)}, u32[]{:S(2)}, u32[]{:S(2)}) %all-to-all-start.1) | async-done | bytes 2080 | tf_op jit(solution)/shard_map/all_to_all | solution.py:136
  35.3 4.5 %all-to-all-start = ((bf16[2,8,32,3072]{3,2,0,1:T(8,128)(2,1)}), bf16[2,8,32,3072]{3,2,0,1:T(8,128)(2,1)}, u32[]{:S(2)}, u32[]{:S(2)}) async-start(bf16[2,8,32,3072]{3,2,0,1:T(8,128)(2,1)} %copy.76), calls=%async_computation | async-start | bytes 6291456 | tf_op jit(solution)/shard_map/all_to_all | solution.py:135
  40.4 73.6 %all-to-all-done = bf16[2,8,32,3072]{3,2,0,1:T(8,128)(2,1)} async-done(((bf16[2,8,32,3072]{3,2,0,1:T(8,128)(2,1)}), bf16[2,8,32,3072]{3,2,0,1:T(8,128)(2,1)}, u32[]{:S(2)}, u32[]{:S(2)}) %all-to-all-start) | async-done | bytes 3145760 | tf_op jit(solution)/shard_map/all_to_all | solution.py:135
  114.0 29.7 %while.47 = (s32[]{:T(128)}, bf16[2,8,32,1024]{3,2,0,1:T(8,128)(2,1)}, bf16[2,8,32,3072]{3,2,0,1:T(8,128)(2,1)}, s32[2,8,32]{2,0,1:T(2,128)S(1)}, s32[]{:T(128)}, /*index=5*/s32[]{:T(128)}, s32[]{:T(128)}) while((s32[]{:T(128)}, bf16[2,8,32,1024]{3,2,0,1:T(8,128)(2,1)}, bf16[2,8,32,3072]{3,2,0,1:T(8,128)(2,1)}, s32[2,8,32]{2,0,1:T(2,128)S(1)}, ...), condition=%wide.region_15.16_spmd, body=%wide.region_10.15_spmd.sunk | while | flops 17628672 | bytes 13550306 | solution.py:132
  114.0 1.6 constant_dynamic-slice_fusion.6
  116.5 9.8 %while.50 = (s32[]{:T(128)}, bf16[16,256,64]{1,2,0:T(8,128)(2,1)S(1)}, bf16[16,256,64]{1,2,0:T(8,128)(2,1)S(1)}, bf16[16,256,64]{1,2,0:T(8,128)(2,1)S(1)}, bf16[...) while((s32[]{:T(128)}, bf16[16,256,64]{1,2,0:T(8,128)(2,1)S(1)}, ...), condition=%wide.region_14.14_spmd.clone, body=%wide.region_11.13_spmd.clone.sunk | while | flops 17628672 | bytes 962637 | solution.py:69
  128.9 1.6 constant_dynamic-slice_fusion.6
  131.3 9.8 %while.50 = (s32[]{:T(128)}, bf16[16,256,64]{1,2,0:T(8,128)(2,1)S(1)}, bf16[16,256,64]{1,2,0:T(8,128)(2,1)S(1)}, bf16[16,256,64]{1,2,0:T(8,128)(2,1)S(1)}, bf16[...) while((s32[]{:T(128)}, bf16[16,256,64]{1,2,0:T(8,128)(2,1)S(1)}, ...), condition=%wide.region_14.14_spmd.clone, body=%wide.region_11.13_spmd.clone.sunk | while | flops 17628672 | bytes 962637 | solution.py:69
  143.7 3.6 %all-to-all-start.2 = ((bf16[2,8,32,1024]{3,2,0,1:T(8,128)(2,1)}), bf16[2,8,32,1024]{3,2,0,1:T(8,128)(2,1)S(1)}, u32[]{:S(2)}, u32[]{:S(2)}) async-start(bf16[2,8,32,1024]{3,2,0,1:T(8,128)(2,1)} %get-tuple-element.187), calls=%async_computation.2 | async-start | bytes 2097152 | tf_op jit(solution)/shard_map/all_to_all | solution.py:139
  147.2 14.3 %while.48 = (s32[]{:T(128)}, f32[16,256,64]{1,2,0:T(8,128)}, f32[16,256]{1,0:T(8,128)S(1)}, f32[256,256]{1,0:T(8,128)S(1)}, bf16[16,256,64]{1,2,0:T(8,128)(2,1)S(1)}, /*index=5*/s32[]{:T(128)}) while((s32[]{:T(128)}, f32[16,256,64]{1,2,0:T(8,128)}, f32[16,256]{1,0:T(8,128)S(1)}, f32[256,256]{1,0:T(8,128)S(1)}, ...), condition=%wide.region_3.4_spmd.clone, body=%wide.region_2.3_spmd.clone.sunk | while | flops 8781826 | bytes 365641 | solution.py:38
  161.6 36.7 %all-gather.1 = f32[64,1,16]{2,1,0:T(1,128)S(1)} all-gather(f32[1,1,16]{2,1,0:T(1,128)S(1)} %bitcast.166), channel_id=1, replica_groups=mesh['tm'=64,'space'=8] {'tm'}, dimensions={0}, use_global_device_ids=true | all-gather | bytes 4160 | tf_op jit(solution)/shard_map/all_gather | solution.py:11
  198.4 77.8 %while.49 = (s32[]{:T(128)}, f32[16,64,128]{2,1,0:T(8,128)S(1)}, s32[]{:T(128)}, f32[64,16]{1,0:T(8,128)S(1)}, f32[64,16,64,128]{3,2,1,0:T(8,128)}, /*index=5*/s32[]{:T(128)}, s32[]{:T(128)}) while((s32[]{:T(128)}, f32[16,64,128]{2,1,0:T(8,128)S(1)}, s32[]{:T(128)}, f32[64,16]{1,0:T(8,128)S(1)}, f32[64,16,64,128]{3,2,1,0:T(8,128)}, ...), condition=%wide.region_5.6_spmd.clone, body=%wide.region_4.5_spmd.clone.sunk | while | flops 524292 | bytes 1573161 | solution.py:21
  198.5 1.3 fusion.61
  199.8 1.2 fusion.61
  201.0 1.2 fusion.61
  202.2 1.2 fusion.61
  203.4 1.2 fusion.61
  204.6 1.2 fusion.61
  205.8 1.2 fusion.61
  207.0 1.2 fusion.61
  208.3 1.2 fusion.61
  209.5 1.2 fusion.61
  210.7 1.2 fusion.61
  211.9 1.2 fusion.61
  213.1 1.2 fusion.61
  214.3 1.2 fusion.61
  216.8 1.2 fusion.61
  218.0 1.2 fusion.61
  219.2 1.2 fusion.61
  220.4 1.2 fusion.61
  222.8 1.2 fusion.61
  225.3 1.2 fusion.61
  227.7 1.2 fusion.61
  230.1 1.2 fusion.61
  232.5 1.2 fusion.61
  235.0 1.2 fusion.61
  237.4 1.2 fusion.61
  239.8 1.2 fusion.61
  241.0 1.2 fusion.61
  242.3 1.2 fusion.61
  243.5 1.2 fusion.61
  245.9 1.2 fusion.61
  248.3 1.2 fusion.61
  250.8 1.2 fusion.61
  253.2 1.2 fusion.61
  255.6 1.2 fusion.61
  258.0 1.2 fusion.61
  260.5 1.2 fusion.61
  262.9 1.2 fusion.61
  264.1 1.2 fusion.61
  265.3 1.2 fusion.61
  266.5 1.2 fusion.61
  269.0 1.2 fusion.61
  271.4 1.2 fusion.61
  273.8 1.2 fusion.61
  278.0 2.7 reshape.96
  280.7 2.3 copy.74
  283.0 2.4 fusion.32
  (280 shorter events, 74.7 us)
Async XLA Ops:
  6.5 22.2 %copy-start = (bf16[2,128,3072]{2,1,0:T(8,128)(2,1)S(1)}, bf16[2,128,3072]{2,1,0:T(8,128)(2,1)}, u32[]{:S(2)}) copy-start(bf16[2,128,3072]{2,1,0:T(8,128)(2,1)} %param.19) | copy-start | bytes 4718596
  6.5 191.9 %all-gather.4.cloned.1.call-start = ((), (), s32[]{:S(2)}) async-start(), calls=%async_computation.3 | async-start | bytes 34078720 | tf_op jit(solution)/shard_map/all_gather | solution.py:11
  9.6 5.8 %copy-start.3 = (bf16[2,128,128]{2,1,0:T(8,128)(2,1)S(1)}, bf16[2,128,128]{2,1,0:T(8,128)(2,1)}, u32[]{:S(2)}) copy-start(bf16[2,128,128]{2,1,0:T(8,128)(2,1)} %param.16) | copy-start | bytes 196612
  11.4 5.2 %copy-start.6 = (s32[2,128]{1,0:T(2,128)S(1)}, s32[2,128]{1,0:T(2,128)}, u32[]{:S(2)}) copy-start(s32[2,128]{1,0:T(2,128)} %param.20) | copy-start | bytes 3076
  17.9 17.4 %all-to-all-start.1 = ((s32[2,8,32]{2,0,1:T(2,128)}), s32[2,8,32]{2,0,1:T(2,128)S(1)}, u32[]{:S(2)}, u32[]{:S(2)}) async-start(s32[2,8,32]{2,0,1:T(2,128)} %copy.77), calls=%async_computation.1 | async-start | bytes 16384 | tf_op jit(solution)/shard_map/all_to_all | solution.py:136
  31.8 8.4 %copy-start.4 = (bf16[2,128,128]{2,1,0:T(8,128)(2,1)S(1)}, bf16[2,128,128]{2,1,0:T(8,128)(2,1)}, u32[]{:S(2)}) copy-start(bf16[2,128,128]{2,1,0:T(8,128)(2,1)} %param.17) | copy-start | bytes 196612
  35.3 78.7 %all-to-all-start = ((bf16[2,8,32,3072]{3,2,0,1:T(8,128)(2,1)}), bf16[2,8,32,3072]{3,2,0,1:T(8,128)(2,1)}, u32[]{:S(2)}, u32[]{:S(2)}) async-start(bf16[2,8,32,3072]{3,2,0,1:T(8,128)(2,1)} %copy.76), calls=%async_computation | async-start | bytes 6291456 | tf_op jit(solution)/shard_map/all_to_all | solution.py:135
  143.7 54.6 %all-to-all-start.2 = ((bf16[2,8,32,1024]{3,2,0,1:T(8,128)(2,1)}), bf16[2,8,32,1024]{3,2,0,1:T(8,128)(2,1)S(1)}, u32[]{:S(2)}, u32[]{:S(2)}) async-start(bf16[2,8,32,1024]{3,2,0,1:T(8,128)(2,1)} %get-tuple-element.187), calls=%async_computation.2 | async-start | bytes 2097152 | tf_op jit(solution)/shard_map/all_to_all | solution.py:139
  198.4 77.8 %copy-start.2 = (f32[16,256,64]{1,2,0:T(8,128)S(1)}, f32[16,256,64]{1,2,0:T(8,128)}, u32[]{:S(2)}) copy-start(f32[16,256,64]{1,2,0:T(8,128)} %get-tuple-element.185) | copy-start | bytes 3145732
  276.9 6.2 %copy-start.5 = (f32[1024]{0:T(1024)S(1)}, f32[1024]{0:T(1024)}, u32[]{:S(2)}) copy-start(f32[1024]{0:T(1024)} %param.21) | copy-start | bytes 12292
  276.9 8.5 %copy-start.1 = (bf16[2,128,3072]{2,1,0:T(8,128)(2,1)S(1)}, bf16[2,128,3072]{2,1,0:T(8,128)(2,1)}, u32[]{:S(2)}) copy-start(bf16[2,128,3072]{2,1,0:T(8,128)(2,1)} %param.19) | copy-start | bytes 4718596
Sparse Core Ops, SparseCore 0:
  16.7 153.5 all-gather.3
where the time goes:
time: 296 us; the launch traced here: 292 us
  other arithmetic  82.8 us (28%)
  waiting for transfers between devices  77.2 us (26%)
  blocking collectives  36.7 us (12%)
  matrix products  35.2 us (12%)
  local copies, waits for them, and re-layouts  25.4 us (9%)
  starting transfers between devices  18.9 us (6%)
  between operations  13.6 us (5%)
    select_n x64, other arithmetic, step(): return jax.tree.map(lambda a, b: jnp.where(reached, a, b), new, before)  75.1 us
    all_to_all x1, waiting for transfers between devices, shards(): lax.all_to_all(send_rows, 'space', split_axis=1, concat_axis=1, tiled=True)  73.6 us
    all_gather x1, blocking collectives, carried_in(): everything = jax.tree.map(lambda part: lax.all_gather(part, axis), x)  36.7 us
    dot_general x16, matrix products, block_one_head(): return jnp.dot(mixing, head_x, preferred_element_type=jnp.float32)  14.2 us
    all_to_all x1, starting transfers between devices, shards(): lax.all_to_all(send_labels, 'space', split_axis=1, concat_axis=1, tiled=T...  10.9 us
    dot_general x32, matrix products, attend_one_head(): jnp.dot(head_q, head_k.T, preferred_element_type=jnp.float32) * scale  8.47 us
    dot_general x32, matrix products, attend_one_head(): return jnp.dot(probs, head_v, preferred_element_type=jnp.float32)  7.21 us
  transfers between devices with their start and end apart: 4, of which 2 were waited for; matrix products, arithmetic and copies ran while one was open for 17% of the time, Pallas kernels for 0%

commit v1 on v0

v1 whole, which is shorter than its diff:
```python
import functools
import math

import jax
import jax.numpy as jnp
from jax import lax
from jax.experimental import pallas as pl
from jax.experimental.pallas import tpu as pltpu
from jax.sharding import PartitionSpec as P

MESH = pl.DeviceIdType.MESH
F32 = jnp.float32
BF16 = jnp.bfloat16
HIGHEST = lax.Precision.HIGHEST

FRAMES = 2
TILE = 128
LANES = 128
ROWS = FRAMES * TILE
STATE = 128
UNIT = STATE // 2
PAD = UNIT + 8


def mixer_kernel(
    pairs, row_len, col_len,
    x_hbm, b_hbm, c_hbm, decay_hbm, qkv_hbm, label_hbm, gain_hbm, out_ref,
    x_ref, b_ref, c_ref, decay_ref, gain_ref, load_sem, qkv_ref, qkv_out, qkv_in, v_ones, label_rows, labels, att, att_out, run_col, run_row, gram, inside, normed,
    state_out, state_in, before, before_decay, total_in, enter_out, entering,
    qkv_send, qkv_recv, label_send, label_recv, state_send, state_recv,
    total_send, total_recv, enter_send, enter_recv, att_send, att_recv,
):
    n_space = pairs
    tm = lax.axis_index("tm")
    z = lax.axis_index("space")
    col = lax.div(tm, row_len)
    j = lax.rem(tm, row_len)
    lane = lax.broadcasted_iota(jnp.int32, (1, LANES), 1)
    first_head = lane < LANES // 2

    def space_peer(d):
        return (tm, lax.rem(z + d, n_space))

    def row_peer(d):
        return (col * row_len + lax.rem(j + d, row_len), z)

    def col_peer(d):
        return (lax.rem(col + d, col_len) * row_len + j, z)

    loads = [
        pltpu.make_async_copy(src, dst, load_sem.at[k])
        for k, (src, dst) in enumerate(
            (
                (qkv_hbm.at[pl.ds(0, TILE)], qkv_ref.at[0]),
                (qkv_hbm.at[pl.ds(TILE, TILE)], qkv_ref.at[1]),
                (label_hbm, labels.at[z]),
                (decay_hbm, decay_ref),
                (x_hbm, x_ref),
                (b_hbm, b_ref),
                (c_hbm, c_ref),
                (gain_hbm, gain_ref),
            )
        )
    ]
    for load in loads:
        load.start()

    barrier = pltpu.get_barrier_semaphore()
    for d in range(1, n_space):
        pl.semaphore_signal(barrier, inc=1, device_id=space_peer(d), device_id_type=MESH)
    for d in range(1, row_len):
        pl.semaphore_signal(barrier, inc=1, device_id=row_peer(d), device_id_type=MESH)
    for d in range(1, col_len):
        pl.semaphore_signal(barrier, inc=1, device_id=col_peer(d), device_id_type=MESH)

    def pack(f):
        loads[f].wait()
        for k in range(3 * n_space):
            qkv_out[f, k] = qkv_ref[f, :, k * LANES : (k + 1) * LANES]
        for part in range(3):
            qkv_in[f, part, z] = qkv_out[f, part * n_space + z]

    pack(0)
    pl.semaphore_wait(barrier, n_space + row_len + col_len - 3)

    def qkv_copy(f, part, d, slot):
        dest = lax.rem(z + d, n_space)
        return pltpu.make_async_remote_copy(
            src_ref=qkv_out.at[f, part * n_space + dest],
            dst_ref=qkv_in.at[f, part, slot],
            send_sem=qkv_send.at[f, part, d],
            recv_sem=qkv_recv.at[f, part, d],
            device_id=space_peer(d),
            device_id_type=MESH,
        )

    def label_copy(d, slot):
        return pltpu.make_async_remote_copy(
            src_ref=label_hbm,
            dst_ref=labels.at[slot],
            send_sem=label_send.at[d],
            recv_sem=label_recv.at[d],
            device_id=space_peer(d),
            device_id_type=MESH,
        )

    order = sorted(range(1, n_space), key=lambda d: -min(d, n_space - d))
    for d in order:
        label_copy(d, z).start()

    def send_qkv(f):
        for part in (1, 2, 0):
            for d in order:
                qkv_copy(f, part, jnp.where(lax.rem(tm, 2) == 0, d, n_space - d), z).start()

    send_qkv(0)
    for load in loads[FRAMES:]:
        load.wait()

    rows_at = lax.broadcasted_iota(jnp.int32, (ROWS, ROWS), 0)
    cols_at = lax.broadcasted_iota(jnp.int32, (ROWS, ROWS), 1)
    tri = jnp.where(cols_at <= rows_at, 1.0, 0.0).astype(F32)
    decay_t = jnp.concatenate([decay_ref[f] for f in range(FRAMES)], axis=1)
    running_t = lax.dot_general(
        decay_t, tri, (((1,), (1,)), ((), ())), precision=HIGHEST, preferred_element_type=F32
    )
    running = jnp.concatenate(
        [running_t, jnp.zeros((LANES - 2 * pairs, ROWS), F32)], axis=0
    ).T
    for h in range(2 * pairs):
        run_col[h] = jnp.broadcast_to(running[:, h : h + 1], (ROWS, LANES))
        run_row[h] = running_t[h : h + 1, :]
    b_t = b_ref[...].astype(F32).T.astype(BF16)

    def state_pair(g, _):
        lanes = pl.ds(pl.multiple_of(g * LANES, LANES), LANES)
        merged = jnp.where(first_head, run_col[2 * g], run_col[2 * g + 1])
        last = merged[ROWS - 1 : ROWS, :]
        weighted = (x_ref[:, lanes].astype(F32) * jnp.exp(last - merged)).astype(BF16)
        local_state = jnp.dot(b_t, weighted, preferred_element_type=F32)
        block_decay = jnp.broadcast_to(jnp.exp(last), (PAD - UNIT, LANES))
        for k in range(2):
            state_out[2 * g + k, 0:UNIT, :] = local_state[k * UNIT : (k + 1) * UNIT]
            state_out[2 * g + k, UNIT:PAD, :] = block_decay
        return 0

    def scan_pair(g, _):
        lanes = pl.ds(pl.multiple_of(g * LANES, LANES), LANES)
        x_pair = x_ref[:, lanes]
        parts = []
        lower = cols_at <= rows_at
        for k in range(2):
            at_t = run_col[2 * g + k]
            spread = jnp.concatenate([at_t] * (ROWS // LANES), axis=1) - run_row[2 * g + k]
            mixing = (gram[...] * jnp.exp(jnp.where(lower, spread, -jnp.inf))).astype(BF16)
            parts.append(jnp.dot(mixing, x_pair, preferred_element_type=F32))
        inside[g] = jnp.where(first_head, parts[0], parts[1])
        return 0

    def state_copy(d, slot):
        return pltpu.make_async_remote_copy(
            src_ref=state_out.at[lax.rem(j + d, row_len)],
            dst_ref=state_in.at[slot],
            send_sem=state_send.at[d],
            recv_sem=state_recv.at[d],
            device_id=row_peer(d),
            device_id_type=MESH,
        )

    def total_copy(d, slot):
        return pltpu.make_async_remote_copy(
            src_ref=total_in.at[col],
            dst_ref=total_in.at[slot],
            send_sem=total_send.at[d],
            recv_sem=total_recv.at[d],
            device_id=col_peer(d),
            device_id_type=MESH,
        )

    def enter_copy(d, slot):
        return pltpu.make_async_remote_copy(
            src_ref=enter_out.at[lax.rem(j + d, row_len)],
            dst_ref=entering.at[slot],
            send_sem=enter_send.at[d],
            recv_sem=enter_recv.at[d],
            device_id=row_peer(d),
            device_id_type=MESH,
        )

    lax.fori_loop(0, pairs, state_pair, 0)
    for d in range(1, row_len):
        state_copy(d, j).start()
    state_in[j] = state_out[j]
    gram[...] = lax.dot_general(
        c_ref[...], b_ref[...], (((1,), (1,)), ((), ())), preferred_element_type=F32
    )
    lax.fori_loop(0, pairs, scan_pair, 0)
    pack(1)
    send_qkv(1)

    def row_prefix():
        for d in range(1, row_len):
            state_copy(d, lax.rem(j - d + row_len, row_len)).wait_recv()

        def step(i, carried):
            state, through = carried
            before[i] = state
            before_decay[i] = through
            here = state_in[i, UNIT:PAD, :]
            return here[0:1] * state + state_in[i, 0:UNIT, :], here * through

        state, through = lax.fori_loop(
            0, row_len, step, (jnp.zeros((UNIT, LANES), F32), jnp.ones((PAD - UNIT, LANES), F32))
        )
        total_in[col, 0:UNIT, :] = state
        total_in[col, UNIT:PAD, :] = through
        for d in range(1, col_len):
            total_copy(d, col).start()

    def col_prefix():
        for d in range(1, col_len):
            total_copy(d, lax.rem(col - d + col_len, col_len)).wait_recv()
        carry = jnp.zeros((UNIT, LANES), F32)
        for i in range(col_len - 1):
            new = total_in[i, UNIT : UNIT + 1, :] * carry + total_in[i, 0:UNIT, :]
            carry = jnp.where(i < col, new, carry)

        def step(i, _):
            enter_out[i] = before[i] + before_decay[i, 0:1, :] * carry
            return 0

        lax.fori_loop(0, row_len, step, 0)
        for d in range(1, row_len):
            enter_copy(d, j).start()
        entering[j] = enter_out[j]

    def finish_scan():
        for d in range(1, row_len):
            enter_copy(d, lax.rem(j - d + row_len, row_len)).wait_recv()
        rows_half = lax.broadcasted_iota(jnp.int32, (LANES, LANES), 0) < LANES // 2
        cols_half = lax.broadcasted_iota(jnp.int32, (LANES, LANES), 1) < LANES // 2
        averager = jnp.where(rows_half == cols_half, 2.0 / LANES, 0.0).astype(F32)

        def norm_pair(g, _):
            state = jnp.concatenate([entering[2 * g], entering[2 * g + 1]], axis=0)
            high = state.astype(BF16)
            low = (state - high.astype(F32)).astype(BF16)
            c_in = c_ref[...]
            carried = jnp.dot(c_in, high, preferred_element_type=F32) + jnp.dot(
                c_in, low, preferred_element_type=F32
            )
            merged = jnp.where(first_head, run_col[2 * g], run_col[2 * g + 1])
            scanned = inside[g] + jnp.exp(merged) * carried
            mean_sq = jnp.dot(
                scanned * scanned, averager, precision=HIGHEST, preferred_element_type=F32
            )
            lanes = pl.ds(pl.multiple_of(g * LANES, LANES), LANES)
            normed[g] = scanned * lax.rsqrt(mean_sq + 1e-05) * gain_ref[:, lanes]
            return 0

        lax.fori_loop(0, pairs, norm_pair, 0)

    def att_copy(f, d, tile, slot):
        return pltpu.make_async_remote_copy(
            src_ref=att_out.at[f, tile],
            dst_ref=att.at[f, slot],
            send_sem=att_send.at[f, d],
            recv_sem=att_recv.at[f, d],
            device_id=space_peer(d),
            device_id_type=MESH,
        )

    def wait_qkv(f, part):
        for d in order:
            qkv_copy(f, part, d, lax.rem(z - d + n_space, n_space)).wait_recv()

    rate = (LANES // 2) ** (-0.5) * math.log2(math.e)
    eye = lax.broadcasted_iota(jnp.int32, (TILE, TILE), 0) == lax.broadcasted_iota(
        jnp.int32, (TILE, TILE), 1
    )

    def attend(f):
        v_ones[:, 0:LANES] = qkv_in[f, 2].reshape(n_space * TILE, LANES)
        label_row = jnp.concatenate(
            [labels[s, f : f + 1, :] for s in range(n_space)], axis=1
        )
        label_rows[...] = label_row.astype(F32)
        keep = [
            jnp.where(first_head, 1.0, 0.0).astype(BF16),
            jnp.where(first_head, 0.0, 1.0).astype(BF16),
        ]

        def step(i, _):
            offsets = (n_space // 2 - i, n_space // 2 + 1 + i)
            tiles = [lax.rem(z + d, n_space) for d in offsets]
            last = i == n_space // 2 - 1

            qkv_copy(f, 0, n_space - offsets[0], tiles[0]).wait_recv()

            @pl.when(jnp.logical_not(last))
            def _():
                qkv_copy(f, 0, n_space - offsets[1], tiles[1]).wait_recv()

            query = [qkv_in[f, 0, tile] for tile in tiles]
            rows = jnp.concatenate([q * k for q in query for k in keep], axis=0)
            keys = qkv_in[f, 1].reshape(n_space * TILE, LANES)
            scores = lax.dot_general(
                rows, keys, (((1,), (1,)), ((), ())), preferred_element_type=F32
            ).reshape(2, 2, TILE, n_space * TILE)
            same = []
            for tile in tiles:
                own_row = labels[tile, f : f + 1, :].astype(F32)
                own_col = jnp.sum(jnp.where(eye, own_row, 0.0), axis=1, keepdims=True)
                same.append((own_col == label_rows[...])[None, None])
            weights = []
            for k in range(2):
                masked = jnp.where(same[k][0], scores[k], -jnp.inf)
                highest = jnp.max(masked, axis=-1, keepdims=True)
                weights.append(jnp.exp2((masked - highest) * rate).astype(BF16))
            summed = jnp.dot(
                jnp.concatenate(weights, axis=0).reshape(4 * TILE, n_space * TILE),
                v_ones[...],
                preferred_element_type=F32,
            ).reshape(2, 2, TILE, 2 * LANES)
            merged = jnp.where(first_head, summed[:, 0, :, 0:LANES], summed[:, 1, :, 0:LANES])
            total = jnp.where(first_head, summed[:, 0, :, LANES:], summed[:, 1, :, LANES:])
            result = (merged / total).astype(BF16)
            for k in range(2):
                att_out[f, tiles[k]] = result[k]
            att_copy(f, offsets[0], tiles[0], z).start()

            @pl.when(jnp.logical_not(last))
            def _():
                att_copy(f, offsets[1], tiles[1], z).start()

            return 0

        lax.fori_loop(0, n_space // 2, step, 0)
        att[f, z] = att_out[f, z]

    v_ones[:, LANES : 2 * LANES] = jnp.ones((n_space * TILE, LANES), BF16)
    row_prefix()
    for d in order:
        label_copy(d, lax.rem(z - d + n_space, n_space)).wait_recv()
    for f in range(FRAMES):
        wait_qkv(f, 1)
        wait_qkv(f, 2)
        attend(f)
        if f == 0:
            col_prefix()
    finish_scan()

    for d in order:
        label_copy(d, z).wait_send()
        for f in range(FRAMES):
            for part in range(3):
                qkv_copy(f, part, d, z).wait_send()
    for d in range(1, row_len):
        state_copy(d, j).wait_send()
        enter_copy(d, j).wait_send()
    for d in range(1, col_len):
        total_copy(d, col).wait_send()

    for f in range(FRAMES):
        for d in range(1, n_space):
            att_copy(f, d, lax.rem(z + d, n_space), lax.rem(z - d + n_space, n_space)).wait_recv()

        def add_pair(g, _):
            lanes = pl.ds(pl.multiple_of(g * LANES, LANES), LANES)
            rows = slice(f * TILE, (f + 1) * TILE)
            out_ref[rows, lanes] = (normed[g, rows, :] + att[f, g].astype(F32)).astype(BF16)
            return 0

        lax.fori_loop(0, pairs, add_pair, 0)

    for f in range(FRAMES):
        for d in order:
            att_copy(f, d, lax.rem(z + d, n_space), z).wait_send()


def hand_on_kernel(src, dst, held, in_sems, out_sems):
    pieces = in_sems.shape[0]
    rows = [pl.ds(k * (ROWS // pieces), ROWS // pieces) for k in range(pieces)]
    reads = [
        pltpu.make_async_copy(src.at[at], held.at[at], in_sems.at[k]) for k, at in enumerate(rows)
    ]
    writes = [
        pltpu.make_async_copy(held.at[at], dst.at[at], out_sems.at[k]) for k, at in enumerate(rows)
    ]
    for read in reads:
        read.start()
    for read, write in zip(reads, writes):
        read.wait()
        write.start()
    for write in writes:
        write.wait()


def solution(mesh):
    n_space = mesh.shape["space"]
    row_len = 16
    col_len = mesh.shape["tm"] // row_len

    def shards(x_in, b_in, c_in, decay_log, qkv, block_of, norm_gain):
        width = x_in.shape[2]
        pairs = width // LANES
        vmem = pl.BlockSpec(memory_space=pltpu.VMEM)
        dma = pltpu.SemaphoreType.DMA
        out = pl.pallas_call(
            functools.partial(mixer_kernel, pairs, row_len, col_len),
            out_shape=jax.ShapeDtypeStruct((ROWS, width), BF16),
            in_specs=[pl.BlockSpec(memory_space=pltpu.HBM)] * 7,
            out_specs=vmem,
            scratch_shapes=[
                pltpu.VMEM((ROWS, width), BF16),
                pltpu.VMEM((ROWS, STATE), BF16),
                pltpu.VMEM((ROWS, STATE), BF16),
                pltpu.VMEM((FRAMES, 2 * pairs, TILE), F32),
                pltpu.VMEM((1, width), F32),
                dma((8,)),
                pltpu.VMEM((FRAMES, TILE, 3 * width), BF16),
                pltpu.VMEM((FRAMES, 3 * pairs, TILE, LANES), BF16),
                pltpu.VMEM((FRAMES, 3, n_space, TILE, LANES), BF16),
                pltpu.VMEM((n_space * TILE, 2 * LANES), BF16),
                pltpu.VMEM((1, n_space * TILE), F32),
                pltpu.VMEM((n_space, FRAMES, TILE), jnp.int32),
                pltpu.VMEM((FRAMES, n_space, TILE, LANES), BF16),
                pltpu.VMEM((FRAMES, n_space, TILE, LANES), BF16),
                pltpu.VMEM((2 * pairs, ROWS, LANES), F32),
                pltpu.VMEM((2 * pairs, 1, ROWS), F32),
                pltpu.VMEM((ROWS, ROWS), F32),
                pltpu.VMEM((pairs, ROWS, LANES), F32),
                pltpu.VMEM((pairs, ROWS, LANES), F32),
                pltpu.VMEM((row_len, PAD, LANES), F32),
                pltpu.VMEM((row_len, PAD, LANES), F32),
                pltpu.VMEM((row_len, UNIT, LANES), F32),
                pltpu.VMEM((row_len, PAD - UNIT, LANES), F32),
                pltpu.VMEM((col_len, PAD, LANES), F32),
                pltpu.VMEM((row_len, UNIT, LANES), F32),
                pltpu.VMEM((row_len, UNIT, LANES), F32),
                dma((FRAMES, 3, n_space)),
                dma((FRAMES, 3, n_space)),
                dma((n_space,)),
                dma((n_space,)),
                dma((row_len,)),
                dma((row_len,)),
                dma((col_len,)),
                dma((col_len,)),
                dma((row_len,)),
                dma((row_len,)),
                dma((FRAMES, n_space)),
                dma((FRAMES, n_space)),
            ],
            compiler_params=pltpu.CompilerParams(
                collective_id=0, has_side_effects=True, vmem_limit_bytes=64 * 1024 * 1024
            ),
        )(
            x_in.reshape(ROWS, width),
            b_in.reshape(ROWS, STATE),
            c_in.reshape(ROWS, STATE),
            jnp.swapaxes(decay_log, 1, 2),
            qkv.reshape(ROWS, 3 * width),
            block_of,
            norm_gain.reshape(1, width),
        )
        hbm = pl.BlockSpec(memory_space=pltpu.HBM)
        out = pl.pallas_call(
            hand_on_kernel,
            out_shape=jax.ShapeDtypeStruct((ROWS, width), BF16),
            in_specs=[hbm],
            out_specs=hbm,
            scratch_shapes=[pltpu.VMEM((ROWS, width), BF16), dma((4,)), dma((4,))],
            compiler_params=pltpu.CompilerParams(vmem_limit_bytes=64 * 1024 * 1024),
        )(out)
        return out.reshape(FRAMES, TILE, width)

    spec = P("tm", "space", None)
    return jax.shard_map(
        shards,
        mesh=mesh,
        in_specs=(spec, spec, spec, spec, spec, P("tm", "space"), P()),
        out_specs=spec,
        check_vma=False,
    )
```

time: 296 us -> 68 us (0.23); the launches traced: 292 us -> 67.9 us
  other arithmetic: 82.8 us -> 0 us
  waiting for transfers between devices: 77.2 us -> 0 us
  Pallas kernels: 0 us -> 67.9 us
  blocking collectives: 36.7 us -> 0 us
  matrix products: 35.2 us -> 0 us
  local copies, waits for them, and re-layouts: 25.4 us -> 0 us
  starting transfers between devices: 18.9 us -> 0 us
  between operations: 13.6 us -> 0.01 us
    all_to_all x3 -> x0, waiting for transfers between devices: 77.2 us -> none  [the longest x1 73.6 us: shards(): lax.all_to_all(send_rows, 'space', split_axis=1, concat_axis=1, tiled=True)]
    select_n x64 -> x0, other arithmetic: 75.1 us -> none  [step(): return jax.tree.map(lambda a, b: jnp.where(reached, a, b), new, before)]
    pallas_call x0 -> x2, Pallas kernels: none -> 67.9 us  [the longest x1 66 us: shards(): pl.pallas_call(functools.partial(mixer_kernel, pairs, row_len, col_len),...]
    all_gather x1 -> x0, blocking collectives: 36.7 us -> none  [carried_in(): everything = jax.tree.map(lambda part: lax.all_gather(part, axis), x)]
    dot_general x85 -> x0, matrix products: 35.2 us -> none  [the longest x16 14.2 us: block_one_head(): return jnp.dot(mixing, head_x, preferred_element_type=jnp.float32)]
    all_to_all x3 -> x0, starting transfers between devices: 18.9 us -> none  [the longest x1 10.9 us: shards(): lax.all_to_all(send_labels, 'space', split_axis=1, concat_axis=1, tiled=T...]
    reshape x5 -> x0, local copies, waits for them, and re-layouts: 8.09 us -> none  [the longest x2 5 us: shards(): (scanned * lax.rsqrt(mean_sq + 1e-05)).reshape(frames_here, tile_len, width)]
    convert_element_type x5 -> x0, local copies, waits for them, and re-layouts: 4.73 us -> none  [the longest x4 3.35 us: attend(): return attended.reshape(query.shape[0], -1).astype(jnp.bfloat16)]
  transfers between devices with their start and end apart: 4 -> 0, of which waited for: 2 -> 0; matrix products, arithmetic and copies ran while one was open for 17% -> 0% of each run, Pallas kernels for 0% -> 0%
where the time goes in v1:
time: 68 us; the launch traced here: 67.9 us
  Pallas kernels  67.9 us (100%)
    pallas_call x1, Pallas kernels, shards(): pl.pallas_call(functools.partial(mixer_kernel, pairs, row_len, col_len),...  66 us
    pallas_call x1, Pallas kernels, shards(): pl.pallas_call(hand_on_kernel, out_shape=jax.ShapeDtypeStruct((ROWS, widt...  1.82 us

profile of v1, /device:TPU:1, one launch (start us, length us, event | category | flops | bytes accessed | tf_op | source)
XLA Modules:
  0.0 67.9 jit_solution(12634892237357333609)
XLA Ops:
  0.0 66.0 %shard_map.73.src = bf16[256,1024]{1,0:T(8,128)(2,1)} custom-call(bf16[256,1024]{1,0:T(8,128)(2,1)} %bitcast.8, bf16[256,128]{1,0:T(8,128)(2,1)} %bitcast.9, bf16[256,128]{1,0:T(8,128)(2,1)} %bitcast.10, f32[2,16,128]{2,1,0:T(8,128)} %bitcast.11, bf16[256,3072]{1,0:T(8,128)(2,1)} %bitcast.7, s32[2,128]{1,0:T(2,128)} %label_hbm.1, f32[1,1024]{1,0:T(1,128)} %bitcast.12), custom_call_target="tpu_custom_call" | custom-call | tf_op jit(solution)/shard_map/pallas_call | solution.py:409
  66.0 1.8 %shard_map.74 = bf16[256,1024]{1,0:T(8,128)(2,1)} custom-call(bf16[256,1024]{1,0:T(8,128)(2,1)} %shard_map.73.src), custom_call_target="tpu_custom_call" | custom-call | tf_op jit(solution)/shard_map/pallas_call | solution.py:467

commit v2 on v1

--- a/solution.py
+++ b/solution.py
@@ -19,16 +19,17 @@
 ROWS = FRAMES * TILE
 STATE = 128
 UNIT = STATE // 2
+CHUNK = 16
 PAD = UNIT + 8
 
 
 def mixer_kernel(
     pairs, row_len, col_len,
-    x_hbm, b_hbm, c_hbm, decay_hbm, qkv_hbm, label_hbm, gain_hbm, out_ref,
-    x_ref, b_ref, c_ref, decay_ref, gain_ref, load_sem, qkv_ref, qkv_out, qkv_in, v_ones, label_rows, labels, att, att_out, run_col, run_row, gram, inside, normed,
+    x_hbm, b_hbm, c_hbm, decay_hbm, qkv_ref, label_hbm, gain_hbm, out_hbm,
+    x_ref, b_ref, c_ref, decay_ref, gain_ref, load_sem, qkv_in, v_ones, label_rows, label_cols, scores, weights, labels, att, att_out, run_col, run_row, gram, inside, normed,
     state_out, state_in, before, before_decay, total_in, enter_out, entering,
     qkv_send, qkv_recv, label_send, label_recv, state_send, state_recv,
-    total_send, total_recv, enter_send, enter_recv, att_send, att_recv,
+    total_send, total_recv, enter_send, enter_recv, att_send, att_recv, here_sem, column_sem, out_ref, out_sem,
 ):
     n_space = pairs
     tm = lax.axis_index("tm")
@@ -51,8 +52,6 @@
         pltpu.make_async_copy(src, dst, load_sem.at[k])
         for k, (src, dst) in enumerate(
             (
-                (qkv_hbm.at[pl.ds(0, TILE)], qkv_ref.at[0]),
-                (qkv_hbm.at[pl.ds(TILE, TILE)], qkv_ref.at[1]),
                 (label_hbm, labels.at[z]),
                 (decay_hbm, decay_ref),
                 (x_hbm, x_ref),
@@ -66,32 +65,57 @@
         load.start()
 
     barrier = pltpu.get_barrier_semaphore()
+    leads = z == 0
     for d in range(1, n_space):
-        pl.semaphore_signal(barrier, inc=1, device_id=space_peer(d), device_id_type=MESH)
-    for d in range(1, row_len):
-        pl.semaphore_signal(barrier, inc=1, device_id=row_peer(d), device_id_type=MESH)
-    for d in range(1, col_len):
-        pl.semaphore_signal(barrier, inc=1, device_id=col_peer(d), device_id_type=MESH)
-
-    def pack(f):
-        loads[f].wait()
-        for k in range(3 * n_space):
-            qkv_out[f, k] = qkv_ref[f, :, k * LANES : (k + 1) * LANES]
-        for part in range(3):
-            qkv_in[f, part, z] = qkv_out[f, part * n_space + z]
-
-    pack(0)
-    pl.semaphore_wait(barrier, n_space + row_len + col_len - 3)
+
+        @pl.when(lax.rem(z + d, n_space) != 0)
+        def _(d=d):
+            pl.semaphore_signal(barrier, inc=1, device_id=space_peer(d), device_id_type=MESH)
+
+    @pl.when(jnp.logical_not(leads))
+    def _():
+        pl.semaphore_wait(barrier, n_space - 1)
+        pl.semaphore_signal(here_sem, inc=1, device_id=(tm, 0), device_id_type=MESH)
+
+    @pl.when(leads)
+    def _():
+        pl.semaphore_wait(here_sem, n_space - 1)
+        for d in range(1, row_len):
+            pl.semaphore_signal(barrier, inc=1, device_id=row_peer(d), device_id_type=MESH)
+        for d in range(1, col_len):
+            pl.semaphore_signal(barrier, inc=1, device_id=col_peer(d), device_id_type=MESH)
+
+    def wait_columns():
+        @pl.when(leads)
+        def _():
+            pl.semaphore_wait(barrier, row_len + col_len - 2)
+            for d in range(1, n_space):
+                pl.semaphore_signal(
+                    column_sem, inc=1, device_id=space_peer(d), device_id_type=MESH
+                )
+
+        @pl.when(jnp.logical_not(leads))
+        def _():
+            pl.semaphore_wait(column_sem, 1)
 
     def qkv_copy(f, part, d, slot):
         dest = lax.rem(z + d, n_space)
+        lanes = pl.ds(pl.multiple_of((part * n_space + dest) * LANES, LANES), LANES)
         return pltpu.make_async_remote_copy(
-            src_ref=qkv_out.at[f, part * n_space + dest],
+            src_ref=qkv_ref.at[pl.ds(f * TILE, TILE), lanes],
             dst_ref=qkv_in.at[f, part, slot],
             send_sem=qkv_send.at[f, part, d],
             recv_sem=qkv_recv.at[f, part, d],
             device_id=space_peer(d),
             device_id_type=MESH,
+        )
+
+    def qkv_own(f, part):
+        lanes = pl.ds(pl.multiple_of((part * n_space + z) * LANES, LANES), LANES)
+        return pltpu.make_async_copy(
+            qkv_ref.at[pl.ds(f * TILE, TILE), lanes],
+            qkv_in.at[f, part, z],
+            qkv_recv.at[f, part, 0],
         )
 
     def label_copy(d, slot):
@@ -104,17 +128,31 @@
             device_id_type=MESH,
         )
 
-    order = sorted(range(1, n_space), key=lambda d: -min(d, n_space - d))
-    for d in order:
-        label_copy(d, z).start()
-
-    def send_qkv(f):
-        for part in (1, 2, 0):
-            for d in order:
-                qkv_copy(f, part, jnp.where(lax.rem(tm, 2) == 0, d, n_space - d), z).start()
-
-    send_qkv(0)
-    for load in loads[FRAMES:]:
+    def each(count, act):
+        def body(i, _):
+            act(i)
+            return 0
+
+        lax.fori_loop(0, count, body, 0)
+
+    def each_offset(act):
+        sign = 1 - 2 * lax.rem(tm, 2)
+        each(
+            n_space - 1,
+            lambda i: act(
+                n_space // 2 + lax.div(i + 1, 2) * (1 - 2 * lax.rem(i, 2)) * sign
+            ),
+        )
+
+    def send_qkv(f, part):
+        each_offset(lambda d: qkv_copy(f, part, d, z).start())
+        qkv_own(f, part).start()
+
+    parts = (1, 2, 0)
+    for part in parts:
+        send_qkv(0, part)
+    each_offset(lambda d: label_copy(d, z).start())
+    for load in loads:
         load.wait()
 
     rows_at = lax.broadcasted_iota(jnp.int32, (ROWS, ROWS), 0)
@@ -132,6 +170,10 @@
         run_row[h] = running_t[h : h + 1, :]
     b_t = b_ref[...].astype(F32).T.astype(BF16)
 
+    low_tile = lax.broadcasted_iota(jnp.int32, (TILE, TILE), 1) <= lax.broadcasted_iota(
+        jnp.int32, (TILE, TILE), 0
+    )
+
     def state_pair(g, _):
         lanes = pl.ds(pl.multiple_of(g * LANES, LANES), LANES)
         merged = jnp.where(first_head, run_col[2 * g], run_col[2 * g + 1])
@@ -147,14 +189,29 @@
     def scan_pair(g, _):
         lanes = pl.ds(pl.multiple_of(g * LANES, LANES), LANES)
         x_pair = x_ref[:, lanes]
-        parts = []
-        lower = cols_at <= rows_at
+        early, late = slice(0, TILE), slice(TILE, 2 * TILE)
+        first, second = [], []
         for k in range(2):
-            at_t = run_col[2 * g + k]
-            spread = jnp.concatenate([at_t] * (ROWS // LANES), axis=1) - run_row[2 * g + k]
-            mixing = (gram[...] * jnp.exp(jnp.where(lower, spread, -jnp.inf))).astype(BF16)
-            parts.append(jnp.dot(mixing, x_pair, preferred_element_type=F32))
-        inside[g] = jnp.where(first_head, parts[0], parts[1])
+            h = 2 * g + k
+
+            def mix(rows, cols, masked):
+                spread = run_col[h, rows, :] - run_row[h, :, cols]
+                if masked:
+                    spread = jnp.where(low_tile, spread, -jnp.inf)
+                return (gram[rows, cols] * jnp.exp(spread)).astype(BF16)
+
+            first.append(mix(early, early, True))
+            second.append(
+                jnp.concatenate([mix(late, early, False), mix(late, late, True)], axis=1)
+            )
+        for rows, mixing, values in (
+            (early, first, x_pair[early]),
+            (late, second, x_pair),
+        ):
+            both = jnp.dot(
+                jnp.concatenate(mixing, axis=0), values, preferred_element_type=F32
+            )
+            inside[g, rows, :] = jnp.where(first_head, both[early], both[late])
         return 0
 
     def state_copy(d, slot):
@@ -188,19 +245,22 @@
         )
 
     lax.fori_loop(0, pairs, state_pair, 0)
-    for d in range(1, row_len):
-        state_copy(d, j).start()
-    state_in[j] = state_out[j]
     gram[...] = lax.dot_general(
         c_ref[...], b_ref[...], (((1,), (1,)), ((), ())), preferred_element_type=F32
     )
     lax.fori_loop(0, pairs, scan_pair, 0)
-    pack(1)
-    send_qkv(1)
+    wait_columns()
+    each(row_len - 1, lambda i: state_copy(i + 1, j).start())
+    state_in[j] = state_out[j]
+    for part in parts:
+        each_offset(lambda d: qkv_copy(0, part, d, z).wait_send())
+        send_qkv(1, part)
 
     def row_prefix():
-        for d in range(1, row_len):
-            state_copy(d, lax.rem(j - d + row_len, row_len)).wait_recv()
+        each(
+            row_len - 1,
+            lambda i: state_copy(i + 1, lax.rem(j - i - 1 + row_len, row_len)).wait_recv(),
+        )
 
         def step(i, carried):
             state, through = carried
@@ -230,13 +290,14 @@
             return 0
 
         lax.fori_loop(0, row_len, step, 0)
-        for d in range(1, row_len):
-            enter_copy(d, j).start()
+        each(row_len - 1, lambda i: enter_copy(i + 1, j).start())
         entering[j] = enter_out[j]
 
     def finish_scan():
-        for d in range(1, row_len):
-            enter_copy(d, lax.rem(j - d + row_len, row_len)).wait_recv()
+        each(
+            row_len - 1,
+            lambda i: enter_copy(i + 1, lax.rem(j - i - 1 + row_len, row_len)).wait_recv(),
+        )
         rows_half = lax.broadcasted_iota(jnp.int32, (LANES, LANES), 0) < LANES // 2
         cols_half = lax.broadcasted_iota(jnp.int32, (LANES, LANES), 1) < LANES // 2
         averager = jnp.where(rows_half == cols_half, 2.0 / LANES, 0.0).astype(F32)
@@ -271,20 +332,18 @@
         )
 
     def wait_qkv(f, part):
-        for d in order:
-            qkv_copy(f, part, d, lax.rem(z - d + n_space, n_space)).wait_recv()
+        each_offset(
+            lambda d: qkv_copy(f, part, d, lax.rem(z - d + n_space, n_space)).wait_recv()
+        )
+        qkv_own(f, part).wait()
 
     rate = (LANES // 2) ** (-0.5) * math.log2(math.e)
-    eye = lax.broadcasted_iota(jnp.int32, (TILE, TILE), 0) == lax.broadcasted_iota(
-        jnp.int32, (TILE, TILE), 1
-    )
-
     def attend(f):
         v_ones[:, 0:LANES] = qkv_in[f, 2].reshape(n_space * TILE, LANES)
-        label_row = jnp.concatenate(
-            [labels[s, f : f + 1, :] for s in range(n_space)], axis=1
-        )
-        label_rows[...] = label_row.astype(F32)
+        for s in range(n_space):
+            row = labels[s, f : f + 1, :].astype(F32)
+            label_rows[:, s * LANES : (s + 1) * LANES] = jnp.broadcast_to(row, (CHUNK, LANES))
+            label_cols[s] = jnp.broadcast_to(row, (TILE, TILE)).T
         keep = [
             jnp.where(first_head, 1.0, 0.0).astype(BF16),
             jnp.where(first_head, 0.0, 1.0).astype(BF16),
@@ -301,26 +360,27 @@
             def _():
                 qkv_copy(f, 0, n_space - offsets[1], tiles[1]).wait_recv()
 
+            @pl.when(last)
+            def _():
+                qkv_own(f, 0).wait()
+
             query = [qkv_in[f, 0, tile] for tile in tiles]
             rows = jnp.concatenate([q * k for q in query for k in keep], axis=0)
             keys = qkv_in[f, 1].reshape(n_space * TILE, LANES)
-            scores = lax.dot_general(
+            scores[...] = lax.dot_general(
                 rows, keys, (((1,), (1,)), ((), ())), preferred_element_type=F32
-            ).reshape(2, 2, TILE, n_space * TILE)
-            same = []
-            for tile in tiles:
-                own_row = labels[tile, f : f + 1, :].astype(F32)
-                own_col = jnp.sum(jnp.where(eye, own_row, 0.0), axis=1, keepdims=True)
-                same.append((own_col == label_rows[...])[None, None])
-            weights = []
+            )
             for k in range(2):
-                masked = jnp.where(same[k][0], scores[k], -jnp.inf)
-                highest = jnp.max(masked, axis=-1, keepdims=True)
-                weights.append(jnp.exp2((masked - highest) * rate).astype(BF16))
+                for c in range(0, TILE, CHUNK):
+                    col = label_cols[tiles[k], c : c + CHUNK, :]
+                    same = jnp.concatenate([col] * n_space, axis=1) == label_rows[...]
+                    for h in range(2):
+                        at = slice((2 * k + h) * TILE + c, (2 * k + h) * TILE + c + CHUNK)
+                        masked = jnp.where(same, scores[at, :], -jnp.inf)
+                        highest = jnp.max(masked, axis=-1, keepdims=True)
+                        weights[at, :] = jnp.exp2((masked - highest) * rate).astype(BF16)
             summed = jnp.dot(
-                jnp.concatenate(weights, axis=0).reshape(4 * TILE, n_space * TILE),
-                v_ones[...],
-                preferred_element_type=F32,
+                weights[...], v_ones[...], preferred_element_type=F32
             ).reshape(2, 2, TILE, 2 * LANES)
             merged = jnp.where(first_head, summed[:, 0, :, 0:LANES], summed[:, 1, :, 0:LANES])
             total = jnp.where(first_head, summed[:, 0, :, LANES:], summed[:, 1, :, LANES:])
@@ -340,8 +400,7 @@
 
     v_ones[:, LANES : 2 * LANES] = jnp.ones((n_space * TILE, LANES), BF16)
     row_prefix()
-    for d in order:
-        label_copy(d, lax.rem(z - d + n_space, n_space)).wait_recv()
+    each_offset(lambda d: label_copy(d, lax.rem(z - d + n_space, n_space)).wait_recv())
     for f in range(FRAMES):
         wait_qkv(f, 1)
         wait_qkv(f, 2)
@@ -350,20 +409,30 @@
             col_prefix()
     finish_scan()
 
-    for d in order:
+    def out_copy(f):
+        rows = pl.ds(f * TILE, TILE)
+        return pltpu.make_async_copy(out_ref.at[rows], out_hbm.at[rows], out_sem.at[f])
+
+    def all_sent(d):
         label_copy(d, z).wait_send()
-        for f in range(FRAMES):
-            for part in range(3):
-                qkv_copy(f, part, d, z).wait_send()
-    for d in range(1, row_len):
-        state_copy(d, j).wait_send()
-        enter_copy(d, j).wait_send()
+        for part in parts:
+            qkv_copy(1, part, d, z).wait_send()
+
+    def states_sent(i):
+        state_copy(i + 1, j).wait_send()
+        enter_copy(i + 1, j).wait_send()
+
+    each_offset(all_sent)
+    each(row_len - 1, states_sent)
     for d in range(1, col_len):
         total_copy(d, col).wait_send()
 
     for f in range(FRAMES):
-        for d in range(1, n_space):
-            att_copy(f, d, lax.rem(z + d, n_space), lax.rem(z - d + n_space, n_space)).wait_recv()
+        each_offset(
+            lambda d: att_copy(
+                f, d, lax.rem(z + d, n_space), lax.rem(z - d + n_space, n_space)
+            ).wait_recv()
+        )
 
         def add_pair(g, _):
             lanes = pl.ds(pl.multiple_of(g * LANES, LANES), LANES)
@@ -372,28 +441,11 @@
             return 0
 
         lax.fori_loop(0, pairs, add_pair, 0)
+        out_copy(f).start()
 
     for f in range(FRAMES):
-        for d in order:
-            att_copy(f, d, lax.rem(z + d, n_space), z).wait_send()
-
-
-def hand_on_kernel(src, dst, held, in_sems, out_sems):
-    pieces = in_sems.shape[0]
-    rows = [pl.ds(k * (ROWS // pieces), ROWS // pieces) for k in range(pieces)]
-    reads = [
-        pltpu.make_async_copy(src.at[at], held.at[at], in_sems.at[k]) for k, at in enumerate(rows)
-    ]
-    writes = [
-        pltpu.make_async_copy(held.at[at], dst.at[at], out_sems.at[k]) for k, at in enumerate(rows)
-    ]
-    for read in reads:
-        read.start()
-    for read, write in zip(reads, writes):
-        read.wait()
-        write.start()
-    for write in writes:
-        write.wait()
+        each_offset(lambda d: att_copy(f, d, lax.rem(z + d, n_space), z).wait_send())
+        out_copy(f).wait()
 
 
 def solution(mesh):
@@ -404,25 +456,25 @@
     def shards(x_in, b_in, c_in, decay_log, qkv, block_of, norm_gain):
         width = x_in.shape[2]
         pairs = width // LANES
-        vmem = pl.BlockSpec(memory_space=pltpu.VMEM)
         dma = pltpu.SemaphoreType.DMA
         out = pl.pallas_call(
             functools.partial(mixer_kernel, pairs, row_len, col_len),
             out_shape=jax.ShapeDtypeStruct((ROWS, width), BF16),
             in_specs=[pl.BlockSpec(memory_space=pltpu.HBM)] * 7,
-            out_specs=vmem,
+            out_specs=pl.BlockSpec(memory_space=pltpu.HBM),
             scratch_shapes=[
                 pltpu.VMEM((ROWS, width), BF16),
                 pltpu.VMEM((ROWS, STATE), BF16),
                 pltpu.VMEM((ROWS, STATE), BF16),
                 pltpu.VMEM((FRAMES, 2 * pairs, TILE), F32),
                 pltpu.VMEM((1, width), F32),
-                dma((8,)),
-                pltpu.VMEM((FRAMES, TILE, 3 * width), BF16),
-                pltpu.VMEM((FRAMES, 3 * pairs, TILE, LANES), BF16),
+                dma((6,)),
                 pltpu.VMEM((FRAMES, 3, n_space, TILE, LANES), BF16),
                 pltpu.VMEM((n_space * TILE, 2 * LANES), BF16),
-                pltpu.VMEM((1, n_space * TILE), F32),
+                pltpu.VMEM((CHUNK, n_space * TILE), F32),
+                pltpu.VMEM((n_space, TILE, TILE), F32),
+                pltpu.VMEM((4 * TILE, n_space * TILE), F32),
+                pltpu.VMEM((4 * TILE, n_space * TILE), BF16),
                 pltpu.VMEM((n_space, FRAMES, TILE), jnp.int32),
                 pltpu.VMEM((FRAMES, n_space, TILE, LANES), BF16),
                 pltpu.VMEM((FRAMES, n_space, TILE, LANES), BF16),
@@ -450,6 +502,10 @@
                 dma((row_len,)),
                 dma((FRAMES, n_space)),
                 dma((FRAMES, n_space)),
+                pltpu.SemaphoreType.REGULAR,
+                pltpu.SemaphoreType.REGULAR,
+                pltpu.VMEM((ROWS, width), BF16),
+                dma((FRAMES,)),
             ],
             compiler_params=pltpu.CompilerParams(
                 collective_id=0, has_side_effects=True, vmem_limit_bytes=64 * 1024 * 1024
@@ -463,15 +519,6 @@
             block_of,
             norm_gain.reshape(1, width),
         )
-        hbm = pl.BlockSpec(memory_space=pltpu.HBM)
-        out = pl.pallas_call(
-            hand_on_kernel,
-            out_shape=jax.ShapeDtypeStruct((ROWS, width), BF16),
-            in_specs=[hbm],
-            out_specs=hbm,
-            scratch_shapes=[pltpu.VMEM((ROWS, width), BF16), dma((4,)), dma((4,))],
-            compiler_params=pltpu.CompilerParams(vmem_limit_bytes=64 * 1024 * 1024),
-        )(out)
         return out.reshape(FRAMES, TILE, width)
 
     spec = P("tm", "space", None)

time: 68 us -> 65.3 us (0.960)
  the two profiles are of different devices: /device:TPU:1 before, /device:TPU:17 now
where the time goes in v2:
time: 65.3 us; the launch traced here: 65.1 us
  Pallas kernels  63.2 us (97%)
  local copies, waits for them, and re-layouts  1.87 us (3%)
    pallas_call x1, Pallas kernels, shards(): pl.pallas_call(functools.partial(mixer_kernel, pairs, row_len, col_len),...  63.2 us
    unnamed x1, local copies, waits for them, and re-layouts  1.87 us

profile of v2, /device:TPU:17, one launch (start us, length us, event | category | flops | bytes accessed | tf_op | source)
XLA Modules:
  0.0 65.1 jit_solution(902626109237564472)
XLA Ops:
  0.0 63.2 %shard_map.73 = bf16[256,1024]{1,0:T(8,128)(2,1)} custom-call(bf16[256,1024]{1,0:T(8,128)(2,1)} %bitcast.9, bf16[256,128]{1,0:T(8,128)(2,1)} %bitcast.10, bf16[256,128]{1,0:T(8,128)(2,1)} %bitcast.11, f32[2,16,128]{2,1,0:T(8,128)} %bitcast.12, bf16[256,3072]{1,0:T(8,128)(2,1)} %bitcast.8, s32[2,128]{1,0:T(2,128)} %label_hbm.1, f32[1,1024]{1,0:T(1,128)} %bitcast.13), custom_call_target="tpu_custom_call" | custom-call | tf_op jit(solution)/shard_map/pallas_call | solution.py:460
  63.2 1.9 %copy.9 = bf16[2,128,1024]{2,1,0:T(8,128)(2,1)} copy(bf16[2,128,1024]{2,1,0:T(8,128)(2,1)} %bitcast.7) | data formatting | bytes 1048576

commit v3 on v2

--- a/solution.py
+++ b/solution.py
@@ -128,30 +128,18 @@
             device_id_type=MESH,
         )
 
-    def each(count, act):
-        def body(i, _):
-            act(i)
-            return 0
-
-        lax.fori_loop(0, count, body, 0)
-
-    def each_offset(act):
-        sign = 1 - 2 * lax.rem(tm, 2)
-        each(
-            n_space - 1,
-            lambda i: act(
-                n_space // 2 + lax.div(i + 1, 2) * (1 - 2 * lax.rem(i, 2)) * sign
-            ),
-        )
+    order = sorted(range(1, n_space), key=lambda d: -min(d, n_space - d))
+    for d in order:
+        label_copy(d, z).start()
 
     def send_qkv(f, part):
-        each_offset(lambda d: qkv_copy(f, part, d, z).start())
+        for far, near in zip(order, reversed(order)):
+            qkv_copy(f, part, jnp.where(lax.rem(tm, 2) == 0, far, near), z).start()
         qkv_own(f, part).start()
 
     parts = (1, 2, 0)
     for part in parts:
         send_qkv(0, part)
-    each_offset(lambda d: label_copy(d, z).start())
     for load in loads:
         load.wait()
 
@@ -250,17 +238,17 @@
     )
     lax.fori_loop(0, pairs, scan_pair, 0)
     wait_columns()
-    each(row_len - 1, lambda i: state_copy(i + 1, j).start())
+    for d in range(1, row_len):
+        state_copy(d, j).start()
     state_in[j] = state_out[j]
     for part in parts:
-        each_offset(lambda d: qkv_copy(0, part, d, z).wait_send())
+        for d in order:
+            qkv_copy(0, part, d, z).wait_send()
         send_qkv(1, part)
 
     def row_prefix():
-        each(
-            row_len - 1,
-            lambda i: state_copy(i + 1, lax.rem(j - i - 1 + row_len, row_len)).wait_recv(),
-        )
+        for d in range(1, row_len):
+            state_copy(d, lax.rem(j - d + row_len, row_len)).wait_recv()
 
         def step(i, carried):
             state, through = carried
@@ -290,14 +278,13 @@
             return 0
 
         lax.fori_loop(0, row_len, step, 0)
-        each(row_len - 1, lambda i: enter_copy(i + 1, j).start())
+        for d in range(1, row_len):
+            enter_copy(d, j).start()
         entering[j] = enter_out[j]
 
     def finish_scan():
-        each(
-            row_len - 1,
-            lambda i: enter_copy(i + 1, lax.rem(j - i - 1 + row_len, row_len)).wait_recv(),
-        )
+        for d in range(1, row_len):
+            enter_copy(d, lax.rem(j - d + row_len, row_len)).wait_recv()
         rows_half = lax.broadcasted_iota(jnp.int32, (LANES, LANES), 0) < LANES // 2
         cols_half = lax.broadcasted_iota(jnp.int32, (LANES, LANES), 1) < LANES // 2
         averager = jnp.where(rows_half == cols_half, 2.0 / LANES, 0.0).astype(F32)
@@ -332,9 +319,8 @@
         )
 
     def wait_qkv(f, part):
-        each_offset(
-            lambda d: qkv_copy(f, part, d, lax.rem(z - d + n_space, n_space)).wait_recv()
-        )
+        for d in order:
+            qkv_copy(f, part, d, lax.rem(z - d + n_space, n_space)).wait_recv()
         qkv_own(f, part).wait()
 
     rate = (LANES // 2) ** (-0.5) * math.log2(math.e)
@@ -400,7 +386,8 @@
 
     v_ones[:, LANES : 2 * LANES] = jnp.ones((n_space * TILE, LANES), BF16)
     row_prefix()
-    each_offset(lambda d: label_copy(d, lax.rem(z - d + n_space, n_space)).wait_recv())
+    for d in order:
+        label_copy(d, lax.rem(z - d + n_space, n_space)).wait_recv()
     for f in range(FRAMES):
         wait_qkv(f, 1)
         wait_qkv(f, 2)
@@ -413,26 +400,19 @@
         rows = pl.ds(f * TILE, TILE)
         return pltpu.make_async_copy(out_ref.at[rows], out_hbm.at[rows], out_sem.at[f])
 
-    def all_sent(d):
+    for d in order:
         label_copy(d, z).wait_send()
         for part in parts:
             qkv_copy(1, part, d, z).wait_send()
-
-    def states_sent(i):
-        state_copy(i + 1, j).wait_send()
-        enter_copy(i + 1, j).wait_send()
-
-    each_offset(all_sent)
-    each(row_len - 1, states_sent)
+    for d in range(1, row_len):
+        state_copy(d, j).wait_send()
+        enter_copy(d, j).wait_send()
     for d in range(1, col_len):
         total_copy(d, col).wait_send()
 
     for f in range(FRAMES):
-        each_offset(
-            lambda d: att_copy(
-                f, d, lax.rem(z + d, n_space), lax.rem(z - d + n_space, n_space)
-            ).wait_recv()
-        )
+        for d in range(1, n_space):
+            att_copy(f, d, lax.rem(z + d, n_space), lax.rem(z - d + n_space, n_space)).wait_recv()
 
         def add_pair(g, _):
             lanes = pl.ds(pl.multiple_of(g * LANES, LANES), LANES)
@@ -444,7 +424,8 @@
         out_copy(f).start()
 
     for f in range(FRAMES):
-        each_offset(lambda d: att_copy(f, d, lax.rem(z + d, n_space), z).wait_send())
+        for d in order:
+            att_copy(f, d, lax.rem(z + d, n_space), z).wait_send()
         out_copy(f).wait()
 
 

time: 65.3 us -> 64.1 us (0.982)
  the two profiles are of different devices: /device:TPU:17 before, /device:TPU:1 now
where the time goes in v3:
time: 64.1 us; the launch traced here: 63.7 us
  Pallas kernels  61.8 us (96%)
  local copies, waits for them, and re-layouts  1.87 us (3%)
    pallas_call x1, Pallas kernels, shards(): pl.pallas_call(functools.partial(mixer_kernel, pairs, row_len, col_len),...  61.8 us
    unnamed x1, local copies, waits for them, and re-layouts  1.87 us

profile of v3, /device:TPU:1, one launch (start us, length us, event | category | flops | bytes accessed | tf_op | source)
XLA Modules:
  0.0 63.7 jit_solution(1356725542924703844)
XLA Ops:
  0.0 61.8 %shard_map.73 = bf16[256,1024]{1,0:T(8,128)(2,1)} custom-call(bf16[256,1024]{1,0:T(8,128)(2,1)} %bitcast.9, bf16[256,128]{1,0:T(8,128)(2,1)} %bitcast.10, bf16[256,128]{1,0:T(8,128)(2,1)} %bitcast.11, f32[2,16,128]{2,1,0:T(8,128)} %bitcast.12, bf16[256,3072]{1,0:T(8,128)(2,1)} %bitcast.8, s32[2,128]{1,0:T(2,128)} %label_hbm.1, f32[1,1024]{1,0:T(1,128)} %bitcast.13), custom_call_target="tpu_custom_call" | custom-call | tf_op jit(solution)/shard_map/pallas_call | solution.py:441
  61.8 1.9 %copy.9 = bf16[2,128,1024]{2,1,0:T(8,128)(2,1)} copy(bf16[2,128,1024]{2,1,0:T(8,128)(2,1)} %bitcast.7) | data formatting | bytes 1048576
